TPU v7x, 32 devices: a whole 2x2x4 slice. The times are simulated.
32 devices in a mesh: seq: 8 (over y, x, core), tp: 4 (over z).
Axes of the slice: x: 2, y: 2, z: 4, core: 2. Of those that a mesh axis runs over, the one named last changes fastest.
Arguments:
- queries: bfloat16 [1024, 4096], P('seq', 'tp'), may hold values from -6 to 6
- suffix_entries: bfloat16 [1024, 4096], P('seq', 'tp'), may hold values from -6 to 6
- prefix_cache: bfloat16 [128, 4096], P(('seq', 'tp')), may hold values from -6 to 6
- block_prefix: int32 [32], replicated, may hold values from 0 to 1, as said below
- request_lengths: int32 [32], P('seq'), may hold values from 0 to 128, as said below
- request_prefix: int32 [32], P('seq'), may hold values from 0 to 1
Outputs:
- attended: bfloat16 [1024, 4096], P('seq', 'tp')
Inputs may be any that keep to these rules, and one draw needn't show every extreme that they name: `request_lengths`: the lengths of one index of seq's requests sum to at most 128; at some index they sum to exactly 128, and there one request alone takes all 128 slots. `block_prefix`: exactly half of the blocks belong to each prefix.
All inputs are finite; a program needn't handle non-finite values.
Results may differ from a plain program's by a relative error of at most 0.0049.
Values may be sent and summed in bfloat16 or wider, within the bound.
A program may use at most 64 MiB of HBM per device.

v0:
```python
import math

import jax
import jax.numpy as jnp
from jax import lax
from jax.sharding import PartitionSpec as P

HEADS = 16
HEAD = 128


masked_score = -1e30
section_rows = 512


def token_layout(lengths, prefixes, slots):
    cumulative = jnp.cumsum(lengths)
    slot_ids = jnp.arange(slots, dtype=jnp.int32)
    request_ids = jnp.sum((slot_ids[:, None] >= cumulative[None, :]).astype(jnp.int32), axis=1)
    live_slots = slot_ids < cumulative[-1]
    onehot = request_ids[:, None] == jnp.arange(lengths.shape[0], dtype=jnp.int32)[None, :]
    token_group = jnp.sum(jnp.where(onehot, prefixes[None, :], 0), axis=1)
    return (slot_ids, request_ids, live_slots, token_group)


def attend(running, query_rows, key_rows, value_rows, allowed):
    old_max, old_total, old_sum = running
    scores = jnp.einsum("thed,rhd->ther", query_rows, key_rows, preferred_element_type=jnp.float32)
    scores = scores * (1.0 / math.sqrt(query_rows.shape[-1]))
    allowed_grid = allowed[:, None, None, :]
    scores = jnp.where(allowed_grid, scores, masked_score)
    new_max = jnp.maximum(old_max, jnp.max(scores, axis=-1))
    rescale = jnp.exp(old_max - new_max)
    weights = jnp.where(allowed_grid, jnp.exp(scores - new_max[..., None]), 0.0)
    new_total = old_total * rescale + jnp.sum(weights, axis=-1)
    products = jnp.einsum(
        "ther,rhd->thed",
        weights.astype(jnp.bfloat16),
        value_rows,
        preferred_element_type=jnp.float32,
    )
    new_sum = old_sum * rescale[..., None] + products
    return (new_max, new_total, new_sum)


def owner_lookup(block_ids, block_prefix):
    match = block_ids[:, None] == jnp.arange(block_prefix.shape[0], dtype=jnp.int32)[None, :]
    return jnp.sum(jnp.where(match, block_prefix[None, :], 0), axis=1)


def empty_state(token_rows, head_count):
    return (
        jnp.full((token_rows, head_count, 2), masked_score, jnp.float32),
        jnp.zeros((token_rows, head_count, 2), jnp.float32),
        jnp.zeros((token_rows, head_count, 2, HEAD), jnp.float32),
    )


def sweep(running, query_rows, rows, head_count, block_of, block_prefix, token_group, live_slots):
    total_rows = rows.shape[0]
    for offset in range(0, total_rows, section_rows):
        row_count = min(section_rows, total_rows - offset)
        section = rows[offset : offset + row_count].reshape(row_count, head_count, 2, HEAD)
        positions = offset + jnp.arange(row_count, dtype=jnp.int32)
        owners = owner_lookup(block_of(positions), block_prefix)
        allowed = (token_group[:, None] == owners[None, :]) & live_slots[:, None]
        running = attend(running, query_rows, section[:, :, 0], section[:, :, 1], allowed)
    return running


def per_device(
    queries, suffix_entries, prefix_cache, block_prefix, request_lengths, request_prefix
):
    tensor_count = lax.axis_size("tp")
    seq_count = lax.axis_size("seq")
    local_heads = HEADS // tensor_count
    token_rows = queries.shape[0]
    block_rows = prefix_cache.shape[0]
    slot_ids, request_ids, live_slots, token_group = token_layout(
        request_lengths, request_prefix, token_rows
    )
    own_query = queries.reshape(token_rows, local_heads, 2, HEAD)
    own_entries = suffix_entries.reshape(token_rows, local_heads, 2, HEAD)
    gathered = lax.all_gather(prefix_cache, "seq", axis=0, tiled=True)
    cached = lax.all_to_all(gathered, "tp", split_axis=1, concat_axis=0, tiled=True)
    span = seq_count * block_rows

    def block_of(positions):
        return positions % span // block_rows * tensor_count + positions // span

    running = sweep(
        empty_state(token_rows, local_heads),
        own_query,
        cached,
        local_heads,
        block_of,
        block_prefix,
        token_group,
        live_slots,
    )
    suffix_allowed = (
        (request_ids[:, None] == request_ids[None, :])
        & (slot_ids[None, :] <= slot_ids[:, None])
        & live_slots[:, None]
    )
    running = attend(running, own_query, own_entries[:, :, 0], own_entries[:, :, 1], suffix_allowed)
    final_max, final_total, final_sum = running
    live_grid = live_slots[:, None, None]
    safe_total = jnp.where(live_grid, final_total, 1.0)
    result = jnp.where(live_grid[..., None], final_sum / safe_total[..., None], 0.0)
    return result.astype(jnp.bfloat16).reshape(token_rows, local_heads * 2 * HEAD)


def solution(mesh):
    in_specs = (P("seq", "tp"), P("seq", "tp"), P(("seq", "tp"), None), P(), P("seq"), P("seq"))
    out_specs = P("seq", "tp")
    return jax.shard_map(
        per_device, mesh=mesh, in_specs=in_specs, out_specs=out_specs, check_vma=False
    )
```

profile of v0, /device:TPU:0, one launch (start us, length us, event | category | flops | bytes accessed | tf_op | source)
XLA Modules:
  0.0 29.0 jit_solution(3131422003055134252)
XLA Ops:
  0.0 11.0 %all-gather = bf16[8,4,4096]{2,1,0:T(4,128)(2,1)S(1)} all-gather(bf16[1,4,4096]{2,1,0:T(4,128)(2,1)} %bitcast.66), channel_id=1, replica_groups=mesh['seq'=8,'tp'=4] {'seq'}, dimensions={0}, use_global_device_ids=true | all-gather | bytes 294912 | tf_op jit(solution)/shard_map/all_gather | solution.py:84
  11.0 0.2 all_to_all.12
  11.2 0.8 %copy.36 = bf16[32,4,1024]{2,0,1:T(8,128)(2,1)} copy(bf16[32,4,1024]{2,1,0:T(4,128)(2,1)S(1)} %all_to_all.12) | data formatting | bytes 524288 | tf_op jit(solution)/shard_map/all_to_all | solution.py:85
  12.0 5.0 %all-to-all-start = ((bf16[32,4,1024]{2,0,1:T(8,128)(2,1)}), bf16[32,4,1024]{2,0,1:T(8,128)(2,1)S(1)}, u32[]{:S(2)}, u32[]{:S(2)}) async-start(bf16[32,4,1024]{2,0,1:T(8,128)(2,1)} %copy.36), calls=%async_computation | async-start | bytes 524288 | tf_op jit(solution)/shard_map/all_to_all | solution.py:85
  17.0 0.6 %copy-done.2 = s32[4]{0:T(128)S(1)} copy-done((s32[4]{0:T(128)S(1)}, s32[4]{0:T(128)}, u32[]{:S(2)}) %copy-start.2) | copy-done | bytes 40
  17.6 0.2 reduce-window.4
  17.8 0.7 %slice.16 = s32[1,1]{0,1:T(1,128)} slice(s32[4,1]{0,1:T(1,128)S(1)} %reduce-window.4), slice={[3:4], [0:1]} | slice | bytes 8 | tf_op jit(solution)/shard_map/slice | solution.py:20
  18.5 0.7 %iota_compare_fusion.4 = pred[128]{0:T(512)(128)(4,1)S(1)} fusion(s32[]{:T(128)} %bitcast.1), kind=kLoop, calls=%fused_computation.56 | loop fusion | flops 128 | bytes 132 | tf_op jit(solution)/shard_map/lt | solution.py:20
  19.3 0.2 reshape.189
  19.4 0.8 %copy-done.1 = bf16[128,1024]{1,0:T(8,128)(2,1)S(1)} copy-done((bf16[128,1024]{1,0:T(8,128)(2,1)S(1)}, bf16[128,1024]{1,0:T(8,128)(2,1)}, u32[]{:S(2)}) %copy-start.1) | copy-done | bytes 262168
  20.2 0.2 copy.41
  20.4 0.5 %copy-done.3 = s32[4]{0:T(128)S(1)} copy-done((s32[4]{0:T(128)S(1)}, s32[4]{0:T(128)}, u32[]{:S(2)}) %copy-start.3) | copy-done | bytes 40
  20.9 0.6 %copy-done.4 = s32[32]{0:T(128)S(1)} copy-done((s32[32]{0:T(128)S(1)}, s32[32]{0:T(128)}, u32[]{:S(2)}) %copy-start.4) | copy-done | bytes 152
  21.6 0.1 compare_and_fusion
  21.7 0.3 fusion.33
  22.0 4.3 %all-to-all-done = bf16[32,4,1024]{2,0,1:T(8,128)(2,1)S(1)} async-done(((bf16[32,4,1024]{2,0,1:T(8,128)(2,1)}), bf16[32,4,1024]{2,0,1:T(8,128)(2,1)S(1)}, u32[]{:S(2)}, u32[]{:S(2)}) %all-to-all-start) | async-done | bytes 262176 | tf_op jit(solution)/shard_map/all_to_all | solution.py:85
  26.3 0.2 reshape.188
  26.5 0.4 %fusion.31 = (bf16[128,4,1,128]{3,2,1,0:T(2,128)(2,1)S(1)}, bf16[128,4,1,128]{3,2,1,0:T(2,128)(2,1)S(1)}) fusion(bf16[128,4,2,128]{3,2,1,0:T(2,128)(2,1)S(1)} %reshape.188), kind=kLoop, calls=%fused_computation.60 | loop fusion | bytes 524288 | tf_op jit(solution)/shard_map/slice | solution.py:67
  26.9 0.2 copy.54
  27.0 0.3 fusion.32
  27.3 0.2 convolution_bitcast_fusion
  27.6 0.2 fusion.10
  27.8 0.3 %fusion.9 = bf16[128,4,2,128]{0,3,2,1:T(8,128)(2,1)S(1)} fusion(f32[128,4,2,128]{0,3,2,1:T(8,128)S(1)} %convolution_bitcast_fusion, f32[128,4,2,128]{0,3,2,1:T(8,128)S(1)} %get-tuple-element.15, f32[128,4,2]{0,2,1:T(2,128)S(1)} %get-tuple-element.5, f32[128,4,2]{0,2,1:T(2,128)S(1)} %get-tuple-element.6, f32[128,4,2]{0,2,1:T(2,128)S(1)} %get-tuple-element.11, ...), kind=kOutput, calls=%fused_computation.13 | convolution fusion | flops 34734080 | bytes 1474688 | tf_op jit(solution)/shard_map/ther,rhd->thed/dot_general | solution.py:36
  28.1 0.9 %copy.46 = bf16[128,1024]{1,0:T(8,128)(2,1)} copy(bf16[128,1024]{0,1:T(8,128)(2,1)S(1)} %bitcast.65) | data formatting | bytes 524288 | tf_op jit(solution)/shard_map/reshape | solution.py:111
  (12 shorter events, 0.3 us)
Async XLA Ops:
  12.0 7.3 %copy-start = (bf16[128,1024]{1,0:T(8,128)(2,1)S(1)}, bf16[128,1024]{1,0:T(8,128)(2,1)}, u32[]{:S(2)}) copy-start(bf16[128,1024]{1,0:T(8,128)(2,1)} %param.6) | copy-start | bytes 786436
  12.0 14.4 %all-to-all-start = ((bf16[32,4,1024]{2,0,1:T(8,128)(2,1)}), bf16[32,4,1024]{2,0,1:T(8,128)(2,1)S(1)}, u32[]{:S(2)}, u32[]{:S(2)}) async-start(bf16[32,4,1024]{2,0,1:T(8,128)(2,1)} %copy.36), calls=%async_computation | async-start | bytes 524288 | tf_op jit(solution)/shard_map/all_to_all | solution.py:85
  17.0 0.7 %copy-start.2 = (s32[4]{0:T(128)S(1)}, s32[4]{0:T(128)}, u32[]{:S(2)}) copy-start(s32[4]{0:T(128)} %param.10) | copy-start | bytes 52
  19.3 1.0 %copy-start.1 = (bf16[128,1024]{1,0:T(8,128)(2,1)S(1)}, bf16[128,1024]{1,0:T(8,128)(2,1)}, u32[]{:S(2)}) copy-start(bf16[128,1024]{1,0:T(8,128)(2,1)} %param.7) | copy-start | bytes 786436
  20.2 0.7 %copy-start.3 = (s32[4]{0:T(128)S(1)}, s32[4]{0:T(128)}, u32[]{:S(2)}) copy-start(s32[4]{0:T(128)} %param.11) | copy-start | bytes 52
  20.9 0.7 %copy-start.4 = (s32[32]{0:T(128)S(1)}, s32[32]{0:T(128)}, u32[]{:S(2)}) copy-start(s32[32]{0:T(128)} %param.9) | copy-start | bytes 388
where the time goes:
time: 29.3 us; the launch traced here: 29 us
  blocking collectives  11 us (38%)
  local copies, waits for them, and re-layouts  6.01 us (21%)
  starting transfers between devices  5 us (17%)
  waiting for transfers between devices  4.33 us (15%)
  other arithmetic  1.49 us (5%)
  matrix products  1.08 us (4%)
    all_gather x1, blocking collectives, per_device(): gathered = lax.all_gather(prefix_cache, 'seq', axis=0, tiled=True)  11 us
    all_to_all x1, starting transfers between devices, per_device(): lax.all_to_all(gathered, 'tp', split_axis=1, concat_axis=0, tiled=True)  5 us
    all_to_all x1, waiting for transfers between devices, per_device(): lax.all_to_all(gathered, 'tp', split_axis=1, concat_axis=0, tiled=True)  4.33 us
    unnamed x12, local copies, waits for them, and re-layouts  2.8 us
    all_to_all x2, local copies, waits for them, and re-layouts, per_device(): lax.all_to_all(gathered, 'tp', split_axis=1, concat_axis=0, tiled=True)  0.99 us
    reshape x1, local copies, waits for them, and re-layouts, per_device(): result.astype(jnp.bfloat16).reshape(token_rows, local_heads * 2 * HEAD)  0.85 us
    lt x1, other arithmetic, token_layout(): live_slots = slot_ids < cumulative[-1]  0.69 us
    slice x1, local copies, waits for them, and re-layouts, token_layout(): live_slots = slot_ids < cumulative[-1]  0.66 us
  transfers between devices with their start and end apart: 1, of which 1 were waited for; matrix products, arithmetic and copies ran while one was open for 9% of the time, Pallas kernels for 0%

commit v1 on v0

v1 whole, which is shorter than its diff:
```python
import functools
import math

import jax
import jax.numpy as jnp
from jax import lax
from jax.experimental import pallas as pl
from jax.experimental.pallas import tpu as pltpu
from jax.sharding import PartitionSpec as P

HEADS = 16
HEAD = 128
PAIR = 2 * HEAD
masked_score = -1e30
MESH = pl.DeviceIdType.MESH


def each(low, high, body):
    if high - low <= 8:
        for index in range(low, high):
            body(index)
    else:
        lax.fori_loop(low, high, lambda index, _: (body(index), 0)[1], 0)


def kernel(
    seq_count,
    tp_count,
    query_hbm,
    entry_hbm,
    cache_hbm,
    owner_hbm,
    length_hbm,
    prefix_hbm,
    out_hbm,
    query,
    entry,
    cache,
    owner,
    length,
    prefix,
    out,
    packed,
    sending,
    stage,
    held,
    peak,
    total,
    load_sem,
    store_sem,
    send_one,
    recv_one,
    send_two,
    recv_two,
):
    s = lax.axis_index("seq")
    t = lax.axis_index("tp")
    slots = query.shape[0]
    heads = query.shape[1] // PAIR
    depth = cache.shape[0]
    rows = heads * depth
    group = tp_count * depth
    scale = math.log2(math.e) / math.sqrt(HEAD)

    loads = [
        pltpu.make_async_copy(source, target, load_sem.at[index])
        for index, (source, target) in enumerate(
            (
                (cache_hbm, cache),
                (entry_hbm, entry),
                (query_hbm, query),
                (length_hbm, length),
                (prefix_hbm, prefix),
                (owner_hbm, owner),
            )
        )
    ]
    for load in loads:
        load.start()

    barrier = pltpu.get_barrier_semaphore()

    def greet_tp(d):
        pl.semaphore_signal(
            barrier, inc=1, device_id=(s, lax.rem(t + d, tp_count)), device_id_type=MESH
        )

    def greet_seq(d):
        pl.semaphore_signal(
            barrier, inc=1, device_id=(lax.rem(s + d, seq_count), t), device_id_type=MESH
        )

    each(1, tp_count, greet_tp)
    each(1, seq_count, greet_seq)

    loads[0].wait()
    for target in range(tp_count):
        for head in range(heads):
            column = (target * heads + head) * PAIR
            packed[target, head * depth : (head + 1) * depth, :] = cache[
                :, column : column + PAIR
            ].astype(jnp.float32)
    sending[...] = packed[...].astype(jnp.bfloat16)
    stage[pl.ds(t, 1)] = sending[pl.ds(t, 1)]

    pl.semaphore_wait(barrier, tp_count + seq_count - 2)

    def step_one(d):
        peer = lax.rem(t + d, tp_count)
        return pltpu.make_async_remote_copy(
            src_ref=sending.at[peer],
            dst_ref=stage.at[t],
            send_sem=send_one.at[d],
            recv_sem=recv_one.at[d],
            device_id=(s, peer),
            device_id_type=MESH,
        )

    def step_two(d):
        return pltpu.make_async_remote_copy(
            src_ref=held.at[s],
            dst_ref=held.at[s],
            send_sem=send_two.at[d],
            recv_sem=recv_two.at[d],
            device_id=(lax.rem(s + d, seq_count), t),
            device_id_type=MESH,
        )

    each(1, tp_count, lambda d: step_one(d).start())
    each(1, tp_count, lambda d: step_one(d).wait_recv())
    for source in range(tp_count):
        piece = stage[source].astype(jnp.float32)
        for head in range(heads):
            packed[head, source * depth : (source + 1) * depth, :] = piece[
                head * depth : (head + 1) * depth
            ]
    held[pl.ds(s, 1)] = packed[...].astype(jnp.bfloat16)[None]
    each(1, seq_count, lambda d: step_two(d).start())

    for load in loads[1:]:
        load.wait()
    row_slot = lax.broadcasted_iota(jnp.int32, (slots, slots), 0)
    key_slot = lax.broadcasted_iota(jnp.int32, (slots, slots), 1)
    row_request = jnp.zeros((slots, slots), jnp.int32)
    key_request = jnp.zeros((slots, slots), jnp.int32)
    token_group = jnp.zeros((slots, HEAD), jnp.int32)
    wide_slot = lax.broadcasted_iota(jnp.int32, (slots, HEAD), 0)
    running = jnp.int32(0)
    for request in range(length.shape[0]):
        token_group = jnp.where(wide_slot >= running, prefix[request], token_group)
        running = running + length[request]
        row_request += (row_slot >= running).astype(jnp.int32)
        key_request += (key_slot >= running).astype(jnp.int32)
    live = wide_slot < running
    suffix_allowed = ((row_request == key_request) & (key_slot <= row_slot))[None]

    ones = jnp.ones((slots, HEAD), jnp.bfloat16)

    def rows_of(head):
        return jnp.concatenate(
            [
                query[:, head * PAIR : head * PAIR + HEAD],
                query[:, head * PAIR + HEAD : (head + 1) * PAIR],
            ],
            axis=0,
        )

    def scores_of(head, keys, allowed):
        scores = lax.dot_general(
            rows_of(head), keys, (((1,), (1,)), ((), ())), preferred_element_type=jnp.float32
        )
        scores = jnp.where(allowed, scores.reshape(2, slots, -1), masked_score)
        return scores.reshape(2 * slots, -1)

    def weigh(scores, top, values):
        weights = jnp.exp2((scores - top) * scale).astype(jnp.bfloat16)
        side = jnp.concatenate([values, jnp.ones_like(values)], axis=1)
        return jnp.dot(weights, side, preferred_element_type=jnp.float32)

    for head in range(heads):
        scores = scores_of(head, entry[:, head * PAIR : head * PAIR + HEAD], suffix_allowed)
        top = jnp.max(scores, axis=1, keepdims=True)
        peak[head] = jnp.broadcast_to(top, (2 * slots, HEAD))
        total[head] = weigh(scores, top, entry[:, head * PAIR + HEAD : (head + 1) * PAIR])

    part = math.gcd(seq_count, 8)
    parts = seq_count // part
    width = part * group
    lane = lax.broadcasted_iota(jnp.int32, (slots, width), 1) // depth

    def allowed_in(index):
        owners = jnp.zeros((slots, width), jnp.int32)
        for block in range(part * tp_count):
            owners = jnp.where(lane == block, owner[index * part * tp_count + block], owners)
        return (token_group[:, :1] == owners)[None]

    def absorb(head, index, allowed):
        block = held[
            pl.ds(index * part, part), head
        ].reshape(width, PAIR)
        scores = scores_of(head, block[:, :HEAD], allowed)
        old = peak[head][:, :1]
        top = jnp.maximum(old, jnp.max(scores, axis=1, keepdims=True))
        return top, total[head] * jnp.exp2((old - top) * scale) + weigh(scores, top, block[:, HEAD:])

    first_allowed = allowed_in(0)
    each(1, seq_count, lambda d: step_two(d).wait_recv())

    def middle(index, _):
        allowed = allowed_in(index)
        for head in range(heads):
            top, new = absorb(head, index, allowed)
            peak[head] = jnp.broadcast_to(top, (2 * slots, HEAD))
            total[head] = new
        return 0

    if parts > 1:
        lax.fori_loop(1, parts, middle, 0)

    stores = []
    for head in range(heads):
        _, new = absorb(head, 0, first_allowed)
        result = new[:, :HEAD] / new[:, HEAD:]
        for expert in range(2):
            column = head * PAIR + expert * HEAD
            out[:, column : column + HEAD] = jnp.where(
                live, result[expert * slots : (expert + 1) * slots], 0.0
            ).astype(jnp.bfloat16)
        columns = pl.ds(head * PAIR, PAIR)
        store = pltpu.make_async_copy(out.at[:, columns], out_hbm.at[:, columns], store_sem.at[head])
        store.start()
        stores.append(store)

    each(1, tp_count, lambda d: step_one(d).wait_send())
    each(1, seq_count, lambda d: step_two(d).wait_send())
    for store in stores:
        store.wait()


def per_device(
    queries, suffix_entries, prefix_cache, block_prefix, request_lengths, request_prefix
):
    tp_count = lax.axis_size("tp")
    seq_count = lax.axis_size("seq")
    slots, columns = queries.shape
    heads = HEADS // tp_count
    depth = prefix_cache.shape[0]
    bf16, f32 = jnp.bfloat16, jnp.float32
    return pl.pallas_call(
        functools.partial(kernel, seq_count, tp_count),
        out_shape=jax.ShapeDtypeStruct((slots, columns), bf16),
        in_specs=[pl.BlockSpec(memory_space=pl.ANY)] * 6,
        out_specs=pl.BlockSpec(memory_space=pl.ANY),
        scratch_shapes=[
            pltpu.VMEM(queries.shape, bf16),
            pltpu.VMEM(suffix_entries.shape, bf16),
            pltpu.VMEM(prefix_cache.shape, bf16),
            pltpu.SMEM(block_prefix.shape, jnp.int32),
            pltpu.SMEM(request_lengths.shape, jnp.int32),
            pltpu.SMEM(request_prefix.shape, jnp.int32),
            pltpu.VMEM((slots, columns), bf16),
            pltpu.VMEM((tp_count, heads * depth, PAIR), f32),
            pltpu.VMEM((tp_count, heads * depth, PAIR), bf16),
            pltpu.VMEM((tp_count, heads * depth, PAIR), bf16),
            pltpu.VMEM((seq_count, heads, tp_count * depth, PAIR), bf16),
            pltpu.VMEM((heads, 2 * slots, HEAD), f32),
            pltpu.VMEM((heads, 2 * slots, PAIR), f32),
            pltpu.SemaphoreType.DMA((6,)),
            pltpu.SemaphoreType.DMA((heads,)),
            pltpu.SemaphoreType.DMA((tp_count,)),
            pltpu.SemaphoreType.DMA((tp_count,)),
            pltpu.SemaphoreType.DMA((seq_count,)),
            pltpu.SemaphoreType.DMA((seq_count,)),
        ],
        compiler_params=pltpu.CompilerParams(
            collective_id=0, has_side_effects=True, vmem_limit_bytes=56 * 1024 * 1024
        ),
    )(queries, suffix_entries, prefix_cache, block_prefix, request_lengths, request_prefix)


def solution(mesh):
    in_specs = (P("seq", "tp"), P("seq", "tp"), P(("seq", "tp"), None), P(), P("seq"), P("seq"))
    out_specs = P("seq", "tp")
    return jax.shard_map(
        per_device, mesh=mesh, in_specs=in_specs, out_specs=out_specs, check_vma=False
    )
```

time: 29.3 us -> 16.2 us (0.55)
  Pallas kernels: 0 us -> 14.3 us
  blocking collectives: 11 us -> 0 us
  starting transfers between devices: 5 us -> 0 us
  local copies, waits for them, and re-layouts: 6.01 us -> 1.67 us
  waiting for transfers between devices: 4.33 us -> 0 us
  other arithmetic: 1.49 us -> 0 us
  matrix products: 1.08 us -> 0 us
    pallas_call x0 -> x1, Pallas kernels: none -> 14.3 us  [per_device(): pl.pallas_call(functools.partial(kernel, seq_count, tp_count), out_shape=...]
    all_gather x1 -> x0, blocking collectives: 11 us -> none  [per_device(): gathered = lax.all_gather(prefix_cache, 'seq', axis=0, tiled=True)]
    all_to_all x1 -> x0, starting transfers between devices: 5 us -> none  [per_device(): lax.all_to_all(gathered, 'tp', split_axis=1, concat_axis=0, tiled=True)]
    all_to_all x1 -> x0, waiting for transfers between devices: 4.33 us -> none  [per_device(): lax.all_to_all(gathered, 'tp', split_axis=1, concat_axis=0, tiled=True)]
    reshape x3 -> x0, local copies, waits for them, and re-layouts: 1.19 us -> none  [the longest x1 0.85 us: per_device(): result.astype(jnp.bfloat16).reshape(token_rows, local_heads * 2 * HEAD)]
    unnamed x12 -> x1, local copies, waits for them, and re-layouts: 2.8 us -> 1.67 us
    dot_general x4 -> x0, matrix products: 1.08 us -> none  [the longest x2 0.55 us: attend(): jnp.einsum('thed,rhd->ther', query_rows, key_rows, preferred_element_type...]
    slice x2 -> x0, local copies, waits for them, and re-layouts: 1.03 us -> none  [the longest x1 0.66 us: token_layout(): live_slots = slot_ids < cumulative[-1]]
  transfers between devices with their start and end apart: 1 -> 0, of which waited for: 1 -> 0; matrix products, arithmetic and copies ran while one was open for 9% -> 0% of each run, Pallas kernels for 0% -> 0%
where the time goes in v1:
time: 16.2 us; the launch traced here: 16 us
  Pallas kernels  14.3 us (88%)
  local copies, waits for them, and re-layouts  1.67 us (10%)
    pallas_call x1, Pallas kernels, per_device(): pl.pallas_call(functools.partial(kernel, seq_count, tp_count), out_shape=...  14.3 us
    unnamed x1, local copies, waits for them, and re-layouts  1.67 us

profile of v1, /device:TPU:0, one launch (start us, length us, event | category | flops | bytes accessed | tf_op | source)
XLA Modules:
  0.0 16.0 jit_solution(2242994653734748566)
XLA Ops:
  0.0 14.3 %shard_map.64 = bf16[128,1024]{1,0:T(8,128)(2,1)} custom-call(bf16[128,1024]{1,0:T(8,128)(2,1)} %query_hbm.1, bf16[128,1024]{1,0:T(8,128)(2,1)} %entry_hbm.1, bf16[4,4096]{1,0:T(4,128)(2,1)} %cache_hbm.1, s32[32]{0:T(128)} %owner_hbm.1, s32[4]{0:T(128)} %length_hbm.1, s32[4]{0:T(128)} %prefix_hbm.1), custom_call_target="tpu_custom_call" | custom-call | tf_op jit(solution)/shard_map/pallas_call | solution.py:249
  14.4 1.7 %copy.8 = bf16[128,1024]{1,0:T(8,128)(2,1)} copy(bf16[128,1024]{1,0:T(8,128)(2,1)} %shard_map.64) | data formatting | bytes 524288

commit v2 on v1

--- a/solution.py
+++ b/solution.py
@@ -32,22 +32,20 @@
     owner_hbm,
     length_hbm,
     prefix_hbm,
-    out_hbm,
+    out,
     query,
     entry,
     cache,
     owner,
     length,
     prefix,
-    out,
     packed,
     sending,
-    stage,
-    held,
+    landed,
+    unpacked,
     peak,
     total,
     load_sem,
-    store_sem,
     send_one,
     recv_one,
     send_two,
@@ -55,10 +53,11 @@
 ):
     s = lax.axis_index("seq")
     t = lax.axis_index("tp")
+    chip, core = s // 2, lax.rem(s, 2)
+    chips = seq_count // 2
     slots = query.shape[0]
     heads = query.shape[1] // PAIR
     depth = cache.shape[0]
-    rows = heads * depth
     group = tp_count * depth
     scale = math.log2(math.e) / math.sqrt(HEAD)
 
@@ -80,18 +79,22 @@
 
     barrier = pltpu.get_barrier_semaphore()
 
-    def greet_tp(d):
-        pl.semaphore_signal(
-            barrier, inc=1, device_id=(s, lax.rem(t + d, tp_count)), device_id_type=MESH
-        )
-
-    def greet_seq(d):
-        pl.semaphore_signal(
-            barrier, inc=1, device_id=(lax.rem(s + d, seq_count), t), device_id_type=MESH
-        )
-
-    each(1, tp_count, greet_tp)
-    each(1, seq_count, greet_seq)
+    def peer(d, e):
+        return (lax.rem(chip + d, chips) * 2 + core, lax.rem(t + e, tp_count))
+
+    other = (chip * 2 + 1 - core, t)
+
+    def pieces(d, body):
+        for e in range(tp_count):
+            if not (isinstance(d, int) and d == 0 and e == 0):
+                body(d, e)
+
+    def greet(d, e):
+        pl.semaphore_signal(barrier, inc=1, device_id=peer(d, e), device_id_type=MESH)
+
+    pl.semaphore_signal(barrier, inc=1, device_id=other, device_id_type=MESH)
+    pieces(0, greet)
+    each(1, chips, lambda d: pieces(d, greet))
 
     loads[0].wait()
     for target in range(tp_count):
@@ -101,41 +104,41 @@
                 :, column : column + PAIR
             ].astype(jnp.float32)
     sending[...] = packed[...].astype(jnp.bfloat16)
-    stage[pl.ds(t, 1)] = sending[pl.ds(t, 1)]
-
-    pl.semaphore_wait(barrier, tp_count + seq_count - 2)
-
-    def step_one(d):
-        peer = lax.rem(t + d, tp_count)
+    landed[0, 0, 0] = sending[pl.ds(t, 1)][0]
+
+    pl.semaphore_wait(barrier, chips * tp_count)
+
+    def direct(d, e):
+        where = peer(d, e)
         return pltpu.make_async_remote_copy(
-            src_ref=sending.at[peer],
-            dst_ref=stage.at[t],
-            send_sem=send_one.at[d],
-            recv_sem=recv_one.at[d],
-            device_id=(s, peer),
+            src_ref=sending.at[where[1]],
+            dst_ref=landed.at[0, d, e],
+            send_sem=send_one.at[d, e],
+            recv_sem=recv_one.at[d, e],
+            device_id=where,
             device_id_type=MESH,
         )
 
-    def step_two(d):
+    def forward(d):
         return pltpu.make_async_remote_copy(
-            src_ref=held.at[s],
-            dst_ref=held.at[s],
+            src_ref=landed.at[0, d],
+            dst_ref=landed.at[1, d],
             send_sem=send_two.at[d],
             recv_sem=recv_two.at[d],
-            device_id=(lax.rem(s + d, seq_count), t),
+            device_id=other,
             device_id_type=MESH,
         )
 
-    each(1, tp_count, lambda d: step_one(d).start())
-    each(1, tp_count, lambda d: step_one(d).wait_recv())
-    for source in range(tp_count):
-        piece = stage[source].astype(jnp.float32)
-        for head in range(heads):
-            packed[head, source * depth : (source + 1) * depth, :] = piece[
-                head * depth : (head + 1) * depth
-            ]
-    held[pl.ds(s, 1)] = packed[...].astype(jnp.bfloat16)[None]
-    each(1, seq_count, lambda d: step_two(d).start())
+    def unpack(side, d):
+        for e in range(tp_count):
+            piece = landed[side, d, e].astype(jnp.float32)
+            for head in range(heads):
+                unpacked[head, side * chips + d, e * depth : (e + 1) * depth, :] = piece[
+                    head * depth : (head + 1) * depth
+                ]
+
+    pieces(0, lambda d, e: direct(d, e).start())
+    each(1, chips, lambda d: pieces(d, lambda d, e: direct(d, e).start()))
 
     for load in loads[1:]:
         load.wait()
@@ -154,8 +157,6 @@
     live = wide_slot < running
     suffix_allowed = ((row_request == key_request) & (key_slot <= row_slot))[None]
 
-    ones = jnp.ones((slots, HEAD), jnp.bfloat16)
-
     def rows_of(head):
         return jnp.concatenate(
             [
@@ -191,20 +192,34 @@
     def allowed_in(index):
         owners = jnp.zeros((slots, width), jnp.int32)
         for block in range(part * tp_count):
-            owners = jnp.where(lane == block, owner[index * part * tp_count + block], owners)
+            place = index * part + block // tp_count
+            side, d = place // chips, place % chips
+            source = (chip - d + chips) % chips * 2 + (core + side) % 2
+            column = (t - block % tp_count + tp_count) % tp_count
+            owners = jnp.where(lane == block, owner[source * tp_count + column], owners)
         return (token_group[:, :1] == owners)[None]
 
     def absorb(head, index, allowed):
-        block = held[
-            pl.ds(index * part, part), head
-        ].reshape(width, PAIR)
+        block = unpacked[head, pl.ds(index * part, part)].reshape(width, PAIR).astype(jnp.bfloat16)
         scores = scores_of(head, block[:, :HEAD], allowed)
         old = peak[head][:, :1]
         top = jnp.maximum(old, jnp.max(scores, axis=1, keepdims=True))
         return top, total[head] * jnp.exp2((old - top) * scale) + weigh(scores, top, block[:, HEAD:])
 
     first_allowed = allowed_in(0)
-    each(1, seq_count, lambda d: step_two(d).wait_recv())
+
+    def pass_on(d):
+        pieces(d, lambda d, e: direct(d, e).wait_recv())
+        forward(d).start()
+        unpack(0, d)
+
+    def take(d):
+        forward(d).wait_recv()
+        unpack(1, d)
+
+    each(0, 1, pass_on)
+    each(1, chips, pass_on)
+    each(0, chips, take)
 
     def middle(index, _):
         allowed = allowed_in(index)
@@ -217,7 +232,6 @@
     if parts > 1:
         lax.fori_loop(1, parts, middle, 0)
 
-    stores = []
     for head in range(heads):
         _, new = absorb(head, 0, first_allowed)
         result = new[:, :HEAD] / new[:, HEAD:]
@@ -226,15 +240,10 @@
             out[:, column : column + HEAD] = jnp.where(
                 live, result[expert * slots : (expert + 1) * slots], 0.0
             ).astype(jnp.bfloat16)
-        columns = pl.ds(head * PAIR, PAIR)
-        store = pltpu.make_async_copy(out.at[:, columns], out_hbm.at[:, columns], store_sem.at[head])
-        store.start()
-        stores.append(store)
-
-    each(1, tp_count, lambda d: step_one(d).wait_send())
-    each(1, seq_count, lambda d: step_two(d).wait_send())
-    for store in stores:
-        store.wait()
+
+    pieces(0, lambda d, e: direct(d, e).wait_send())
+    each(1, chips, lambda d: pieces(d, lambda d, e: direct(d, e).wait_send()))
+    each(0, chips, lambda d: forward(d).wait_send())
 
 
 def per_device(
@@ -248,9 +257,9 @@
     bf16, f32 = jnp.bfloat16, jnp.float32
     return pl.pallas_call(
         functools.partial(kernel, seq_count, tp_count),
-        out_shape=jax.ShapeDtypeStruct((slots, columns), bf16),
+        out_shape=pltpu.VMEM((slots, columns), bf16),
         in_specs=[pl.BlockSpec(memory_space=pl.ANY)] * 6,
-        out_specs=pl.BlockSpec(memory_space=pl.ANY),
+        out_specs=pl.BlockSpec(memory_space=pltpu.VMEM),
         scratch_shapes=[
             pltpu.VMEM(queries.shape, bf16),
             pltpu.VMEM(suffix_entries.shape, bf16),
@@ -258,19 +267,17 @@
             pltpu.SMEM(block_prefix.shape, jnp.int32),
             pltpu.SMEM(request_lengths.shape, jnp.int32),
             pltpu.SMEM(request_prefix.shape, jnp.int32),
-            pltpu.VMEM((slots, columns), bf16),
             pltpu.VMEM((tp_count, heads * depth, PAIR), f32),
             pltpu.VMEM((tp_count, heads * depth, PAIR), bf16),
-            pltpu.VMEM((tp_count, heads * depth, PAIR), bf16),
-            pltpu.VMEM((seq_count, heads, tp_count * depth, PAIR), bf16),
+            pltpu.VMEM((2, seq_count // 2, tp_count, heads * depth, PAIR), bf16),
+            pltpu.VMEM((heads, seq_count, tp_count * depth, PAIR), f32),
             pltpu.VMEM((heads, 2 * slots, HEAD), f32),
             pltpu.VMEM((heads, 2 * slots, PAIR), f32),
             pltpu.SemaphoreType.DMA((6,)),
-            pltpu.SemaphoreType.DMA((heads,)),
-            pltpu.SemaphoreType.DMA((tp_count,)),
-            pltpu.SemaphoreType.DMA((tp_count,)),
-            pltpu.SemaphoreType.DMA((seq_count,)),
-            pltpu.SemaphoreType.DMA((seq_count,)),
+            pltpu.SemaphoreType.DMA((seq_count // 2, tp_count)),
+            pltpu.SemaphoreType.DMA((seq_count // 2, tp_count)),
+            pltpu.SemaphoreType.DMA((seq_count // 2,)),
+            pltpu.SemaphoreType.DMA((seq_count // 2,)),
         ],
         compiler_params=pltpu.CompilerParams(
             collective_id=0, has_side_effects=True, vmem_limit_bytes=56 * 1024 * 1024

time: 16.2 us -> 13.8 us (0.85)
  the two profiles are of different devices: /device:TPU:0 before, /device:TPU:1 now
where the time goes in v2:
time: 13.8 us; the launch traced here: 13.6 us
  Pallas kernels  12.9 us (93%)
  local copies, waits for them, and re-layouts  0.71 us (5%)
    pallas_call x1, Pallas kernels, per_device(): pl.pallas_call(functools.partial(kernel, seq_count, tp_count), out_shape=...  12.9 us
    unnamed x1, local copies, waits for them, and re-layouts  0.71 us

profile of v2, /device:TPU:1, one launch (start us, length us, event | category | flops | bytes accessed | tf_op | source)
XLA Modules:
  0.0 13.6 jit_solution(15469044690669895684)
XLA Ops:
  0.0 12.9 %shard_map.64 = bf16[128,1024]{1,0:T(8,128)(2,1)S(1)} custom-call(bf16[128,1024]{1,0:T(8,128)(2,1)} %query_hbm.1, bf16[128,1024]{1,0:T(8,128)(2,1)} %entry_hbm.1, bf16[4,4096]{1,0:T(4,128)(2,1)} %cache_hbm.1, s32[32]{0:T(128)} %owner_hbm.1, s32[4]{0:T(128)} %length_hbm.1, s32[4]{0:T(128)} %prefix_hbm.1), custom_call_target="tpu_custom_call" | custom-call | tf_op jit(solution)/shard_map/pallas_call | solution.py:258
  12.9 0.7 %copy.8 = bf16[128,1024]{1,0:T(8,128)(2,1)} copy(bf16[128,1024]{1,0:T(8,128)(2,1)S(1)} %shard_map.64) | data formatting | bytes 524288

commit v3 on v2

--- a/solution.py
+++ b/solution.py
@@ -50,6 +50,7 @@
     recv_one,
     send_two,
     recv_two,
+    ready,
 ):
     s = lax.axis_index("seq")
     t = lax.axis_index("tp")
@@ -60,6 +61,35 @@
     depth = cache.shape[0]
     group = tp_count * depth
     scale = math.log2(math.e) / math.sqrt(HEAD)
+
+    barrier = pltpu.get_barrier_semaphore()
+
+    def peer(d, e):
+        return (lax.rem(chip + d, chips) * 2 + core, lax.rem(t + e, tp_count))
+
+    other = (chip * 2 + 1 - core, t)
+
+    def pieces(d, body):
+        for e in range(tp_count):
+            if not (isinstance(d, int) and d == 0 and e == 0):
+                body(d, e)
+
+    place_here = t * chips + chip
+
+    def place_of(d, e):
+        return lax.rem(t + e, tp_count) * chips + lax.rem(chip + d, chips)
+
+    def greet(d, e):
+        @pl.when(place_of(d, e) > place_here)
+        def _():
+            pl.semaphore_signal(barrier, inc=1, device_id=peer(d, e), device_id_type=MESH)
+
+    @pl.when(core == 0)
+    def _():
+        pl.semaphore_signal(barrier, inc=1, device_id=other, device_id_type=MESH)
+
+    pieces(0, greet)
+    each(1, chips, lambda d: pieces(d, greet))
 
     loads = [
         pltpu.make_async_copy(source, target, load_sem.at[index])
@@ -77,25 +107,6 @@
     for load in loads:
         load.start()
 
-    barrier = pltpu.get_barrier_semaphore()
-
-    def peer(d, e):
-        return (lax.rem(chip + d, chips) * 2 + core, lax.rem(t + e, tp_count))
-
-    other = (chip * 2 + 1 - core, t)
-
-    def pieces(d, body):
-        for e in range(tp_count):
-            if not (isinstance(d, int) and d == 0 and e == 0):
-                body(d, e)
-
-    def greet(d, e):
-        pl.semaphore_signal(barrier, inc=1, device_id=peer(d, e), device_id_type=MESH)
-
-    pl.semaphore_signal(barrier, inc=1, device_id=other, device_id_type=MESH)
-    pieces(0, greet)
-    each(1, chips, lambda d: pieces(d, greet))
-
     loads[0].wait()
     for target in range(tp_count):
         for head in range(heads):
@@ -106,39 +117,71 @@
     sending[...] = packed[...].astype(jnp.bfloat16)
     landed[0, 0, 0] = sending[pl.ds(t, 1)][0]
 
-    pl.semaphore_wait(barrier, chips * tp_count)
+    @pl.when(place_here + core > 0)
+    def _():
+        pl.semaphore_wait(barrier, place_here + core)
+
+    def answer(d, e):
+        @pl.when(place_of(d, e) < place_here)
+        def _():
+            pl.semaphore_signal(
+                ready.at[lax.rem(chips - d, chips), lax.rem(tp_count - e, tp_count)],
+                inc=1,
+                device_id=peer(d, e),
+                device_id_type=MESH,
+            )
+
+    @pl.when(core == 1)
+    def _():
+        pl.semaphore_signal(ready.at[0, 0], inc=1, device_id=other, device_id_type=MESH)
+
+    pieces(0, answer)
+    each(1, chips, lambda d: pieces(d, answer))
 
     def direct(d, e):
         where = peer(d, e)
         return pltpu.make_async_remote_copy(
             src_ref=sending.at[where[1]],
-            dst_ref=landed.at[0, d, e],
+            dst_ref=landed.at[0, e, d],
             send_sem=send_one.at[d, e],
             recv_sem=recv_one.at[d, e],
             device_id=where,
             device_id_type=MESH,
         )
 
-    def forward(d):
+    def forward(e):
         return pltpu.make_async_remote_copy(
-            src_ref=landed.at[0, d],
-            dst_ref=landed.at[1, d],
-            send_sem=send_two.at[d],
-            recv_sem=recv_two.at[d],
+            src_ref=landed.at[0, e],
+            dst_ref=landed.at[1, e],
+            send_sem=send_two.at[e],
+            recv_sem=recv_two.at[e],
             device_id=other,
             device_id_type=MESH,
         )
 
-    def unpack(side, d):
-        for e in range(tp_count):
-            piece = landed[side, d, e].astype(jnp.float32)
+    def unpack(side, e):
+        def one(d):
+            piece = landed[side, e, d].astype(jnp.float32)
             for head in range(heads):
                 unpacked[head, side * chips + d, e * depth : (e + 1) * depth, :] = piece[
                     head * depth : (head + 1) * depth
                 ]
 
-    pieces(0, lambda d, e: direct(d, e).start())
-    each(1, chips, lambda d: pieces(d, lambda d, e: direct(d, e).start()))
+        each(0, chips, one)
+
+    def send_back(d, e):
+        @pl.when(place_of(d, e) < place_here)
+        def _():
+            direct(d, e).start()
+
+    def send_on(d, e):
+        @pl.when(place_of(d, e) > place_here)
+        def _():
+            pl.semaphore_wait(ready.at[d, e], 1)
+            direct(d, e).start()
+
+    pieces(0, send_back)
+    each(1, chips, lambda d: pieces(d, send_back))
 
     for load in loads[1:]:
         load.wait()
@@ -178,11 +221,16 @@
         side = jnp.concatenate([values, jnp.ones_like(values)], axis=1)
         return jnp.dot(weights, side, preferred_element_type=jnp.float32)
 
-    for head in range(heads):
+    def suffix(head):
         scores = scores_of(head, entry[:, head * PAIR : head * PAIR + HEAD], suffix_allowed)
         top = jnp.max(scores, axis=1, keepdims=True)
         peak[head] = jnp.broadcast_to(top, (2 * slots, HEAD))
         total[head] = weigh(scores, top, entry[:, head * PAIR + HEAD : (head + 1) * PAIR])
+
+    for e in range(tp_count):
+        each(1 if e == 0 else 0, chips, lambda d: send_on(d, e))
+        for head in range(e * heads // tp_count, (e + 1) * heads // tp_count):
+            suffix(head)
 
     part = math.gcd(seq_count, 8)
     parts = seq_count // part
@@ -202,30 +250,31 @@
     def absorb(head, index, allowed):
         block = unpacked[head, pl.ds(index * part, part)].reshape(width, PAIR).astype(jnp.bfloat16)
         scores = scores_of(head, block[:, :HEAD], allowed)
-        old = peak[head][:, :1]
+        old = peak[head]
         top = jnp.maximum(old, jnp.max(scores, axis=1, keepdims=True))
-        return top, total[head] * jnp.exp2((old - top) * scale) + weigh(scores, top, block[:, HEAD:])
+        factor = jnp.exp2((old - top) * scale)
+        factor = jnp.concatenate([factor, factor], axis=1)
+        return top, total[head] * factor + weigh(scores, top[:, : scores.shape[1]], block[:, HEAD:])
 
     first_allowed = allowed_in(0)
 
-    def pass_on(d):
-        pieces(d, lambda d, e: direct(d, e).wait_recv())
-        forward(d).start()
-        unpack(0, d)
-
-    def take(d):
-        forward(d).wait_recv()
-        unpack(1, d)
-
-    each(0, 1, pass_on)
-    each(1, chips, pass_on)
-    each(0, chips, take)
+    @pl.when(core == 0)
+    def _():
+        pl.semaphore_wait(ready.at[0, 0], 1)
+
+    for e in range(tp_count):
+        each(1 if e == 0 else 0, chips, lambda d: direct(d, e).wait_recv())
+        forward(e).start()
+        unpack(0, e)
+    for e in range(tp_count):
+        forward(e).wait_recv()
+        unpack(1, e)
 
     def middle(index, _):
         allowed = allowed_in(index)
         for head in range(heads):
             top, new = absorb(head, index, allowed)
-            peak[head] = jnp.broadcast_to(top, (2 * slots, HEAD))
+            peak[head] = top
             total[head] = new
         return 0
 
@@ -243,7 +292,8 @@
 
     pieces(0, lambda d, e: direct(d, e).wait_send())
     each(1, chips, lambda d: pieces(d, lambda d, e: direct(d, e).wait_send()))
-    each(0, chips, lambda d: forward(d).wait_send())
+    for e in range(tp_count):
+        forward(e).wait_send()
 
 
 def per_device(
@@ -269,15 +319,16 @@
             pltpu.SMEM(request_prefix.shape, jnp.int32),
             pltpu.VMEM((tp_count, heads * depth, PAIR), f32),
             pltpu.VMEM((tp_count, heads * depth, PAIR), bf16),
-            pltpu.VMEM((2, seq_count // 2, tp_count, heads * depth, PAIR), bf16),
+            pltpu.VMEM((2, tp_count, seq_count // 2, heads * depth, PAIR), bf16),
             pltpu.VMEM((heads, seq_count, tp_count * depth, PAIR), f32),
             pltpu.VMEM((heads, 2 * slots, HEAD), f32),
             pltpu.VMEM((heads, 2 * slots, PAIR), f32),
             pltpu.SemaphoreType.DMA((6,)),
             pltpu.SemaphoreType.DMA((seq_count // 2, tp_count)),
             pltpu.SemaphoreType.DMA((seq_count // 2, tp_count)),
-            pltpu.SemaphoreType.DMA((seq_count // 2,)),
-            pltpu.SemaphoreType.DMA((seq_count // 2,)),
+            pltpu.SemaphoreType.DMA((tp_count,)),
+            pltpu.SemaphoreType.DMA((tp_count,)),
+            pltpu.SemaphoreType.REGULAR((seq_count // 2, tp_count)),
         ],
         compiler_params=pltpu.CompilerParams(
             collective_id=0, has_side_effects=True, vmem_limit_bytes=56 * 1024 * 1024

time: 13.8 us -> 13.2 us (0.957)
  the two profiles are of different devices: /device:TPU:1 before, /device:TPU:25 now
where the time goes in v3:
time: 13.2 us; the launch traced here: 13 us
  Pallas kernels  12.3 us (93%)
  local copies, waits for them, and re-layouts  0.71 us (5%)
    pallas_call x1, Pallas kernels, per_device(): pl.pallas_call(functools.partial(kernel, seq_count, tp_count), out_shape=...  12.3 us
    unnamed x1, local copies, waits for them, and re-layouts  0.71 us

profile of v3, /device:TPU:25, one launch (start us, length us, event | category | flops | bytes accessed | tf_op | source)
XLA Modules:
  0.0 13.0 jit_solution(6867867170927221693)
XLA Ops:
  0.0 12.3 %shard_map.64 = bf16[128,1024]{1,0:T(8,128)(2,1)S(1)} custom-call(bf16[128,1024]{1,0:T(8,128)(2,1)} %query_hbm.1, bf16[128,1024]{1,0:T(8,128)(2,1)} %entry_hbm.1, bf16[4,4096]{1,0:T(4,128)(2,1)} %cache_hbm.1, s32[32]{0:T(128)} %owner_hbm.1, s32[4]{0:T(128)} %length_hbm.1, s32[4]{0:T(128)} %prefix_hbm.1), custom_call_target="tpu_custom_call" | custom-call | tf_op jit(solution)/shard_map/pallas_call | solution.py:308
  12.3 0.7 %copy.8 = bf16[128,1024]{1,0:T(8,128)(2,1)} copy(bf16[128,1024]{1,0:T(8,128)(2,1)S(1)} %shard_map.64) | data formatting | bytes 524288
